TPU v7x, 32 devices: a whole 2x2x4 slice. The times are simulated.
32 devices in a mesh: chan: 8 (over z, y), win: 4 (over x, core).
Axes of the slice: x: 2, y: 2, z: 4, core: 2. Of those that a mesh axis runs over, the one named last changes fastest.
Arguments:
- strain: float32 [64, 32, 7500], P('chan', 'win'), may hold values from -800 to 800
- sources: int32 [4, 8], replicated, may hold values from 0 to 63, as said below
Outputs:
- stacks: float32 [32, 64, 513], P('win', 'chan')
Inputs may be any that keep to these rules, and one draw needn't show every extreme that they name: `sources`: counting channels in aligned blocks of 8, the 8 channels of one round lie in different blocks, and over all rounds every block holds exactly 4 of them.
All inputs are finite; a program needn't handle non-finite values.
Results may differ from a plain program's by a relative error of at most 0.0024.
Values may be sent and summed in bfloat16 or wider, within the bound.
A program may use at most 128 MiB of HBM per device.

v0:
```python
import math

import jax
import jax.numpy as jnp
from jax import lax
from jax.sharding import PartitionSpec as P

MAX_LAG = 256


def whiten(strain):
    mean_square = jnp.mean(strain * strain, axis=-1, keepdims=True)
    return (strain * lax.rsqrt(mean_square + 1e-06)).astype(jnp.bfloat16)


def make_tables(block_len, lag_count):
    frame = 2 * block_len
    step = 2.0 * math.pi / frame
    times = jnp.arange(frame, dtype=jnp.int32)[:, None]
    freqs = jnp.arange(block_len, dtype=jnp.int32)[None, :]
    phase = (times * freqs % frame).astype(jnp.float32) * step
    alternate = jnp.where(times % 2 == 0, 1.0, -1.0).astype(jnp.float32)
    cos_part = jnp.cos(phase)
    sin_part = jnp.where(freqs == 0, alternate, -jnp.sin(phase))
    forward = jnp.concatenate([cos_part, sin_part], axis=1)
    lag_index = jnp.arange(lag_count, dtype=jnp.int32)[None, :]
    freq_col = jnp.arange(block_len, dtype=jnp.int32)[:, None]
    lag_phase = (freq_col * lag_index % frame).astype(jnp.float32) * step
    lag_sign = jnp.where(lag_index % 2 == 0, 1.0, -1.0).astype(jnp.float32)
    first = jnp.where(freq_col == 0, 1.0, 2.0 * jnp.cos(lag_phase))
    second = jnp.where(freq_col == 0, lag_sign, 2.0 * jnp.cos(lag_phase))
    third = jnp.where(freq_col == 0, 0.0, 2.0 * jnp.sin(lag_phase))
    inverse = jnp.concatenate([first, second, third], axis=0) / frame
    return (forward, inverse)


def on_device(strain, sources):
    channels, windows, samples = strain.shape
    rounds, per_round = sources.shape
    block_len = 512
    lag_count = 2 * MAX_LAG + 1
    blocks = -(-samples // block_len)
    whitened = whiten(strain)
    forward, inverse = make_tables(block_len, lag_count)
    factor = 1.0 / math.sqrt(lax.axis_size("win") * windows * samples)
    shard_start = lax.axis_index("chan") * channels
    flat_sources = sources.reshape(-1)
    total_sources = rounds * per_round
    per_win = total_sources // lax.axis_size("win")
    receiver_blocks = jnp.pad(whitened, ((0, 0), (0, 0), (0, blocks * block_len - samples)))
    receiver_blocks = receiver_blocks.reshape(channels, windows * blocks, block_len).astype(
        jnp.float32
    )
    receiver_spec = jnp.dot(
        receiver_blocks,
        forward[:block_len],
        precision=lax.Precision.HIGHEST,
        preferred_element_type=jnp.float32,
    )
    recv_real = receiver_spec[:, :, :block_len]
    recv_imag = receiver_spec[:, :, block_len:]
    per_shard = total_sources // lax.axis_size("chan")
    owner = flat_sources // channels
    position = jnp.arange(total_sources)
    earlier = (owner[None, :] == owner[:, None]) & (position[None, :] < position[:, None])
    rank = jnp.sum(earlier.astype(jnp.int32), axis=1)
    mine = owner == lax.axis_index("chan")
    slot_pick = (mine[None, :] & (rank[None, :] == jnp.arange(per_shard)[:, None])).astype(
        jnp.int32
    )
    local_channel = jnp.sum(slot_pick * (flat_sources - shard_start)[None, :], axis=1)
    one_hot = (local_channel[:, None] == jnp.arange(channels)[None, :]).astype(jnp.bfloat16)
    picked = jnp.einsum(
        "kc,cwt->kwt", one_hot, whitened, preferred_element_type=jnp.float32
    ).astype(jnp.bfloat16)
    gathered = lax.all_gather(picked, "chan", axis=0, tiled=True)
    target = owner * per_shard + rank
    reorder = (target[:, None] == jnp.arange(gathered.shape[0])[None, :]).astype(jnp.bfloat16)
    every_probe = jnp.einsum(
        "sj,jwt->swt", reorder, gathered, preferred_element_type=jnp.float32
    ).astype(jnp.bfloat16)
    results = []
    for round_index in range(rounds):
        probes = every_probe[round_index * per_round : (round_index + 1) * per_round]
        count = probes.shape[0]
        extent = (blocks + 1) * block_len
        padded = jnp.pad(probes, ((0, 0), (0, 0), (MAX_LAG, extent - MAX_LAG - samples)))
        pieces = padded.reshape(count, windows, blocks + 1, block_len)
        segments = jnp.concatenate([pieces[:, :, :-1, :], pieces[:, :, 1:, :]], axis=-1)
        segments = segments.reshape(count, windows * blocks, 2 * block_len).astype(jnp.float32)
        probe_spec = jnp.dot(
            segments, forward, precision=lax.Precision.HIGHEST, preferred_element_type=jnp.float32
        )
        probe_real = probe_spec[:, :, :block_len][:, None]
        probe_imag = probe_spec[:, :, block_len:][:, None]
        both_real = jnp.sum(probe_real * recv_real[None], axis=2)
        both_imag = jnp.sum(probe_imag * recv_imag[None], axis=2)
        cross_one = jnp.sum(probe_imag * recv_real[None], axis=2)
        cross_two = jnp.sum(probe_real * recv_imag[None], axis=2)
        spectra = jnp.concatenate([both_real, both_imag, cross_two - cross_one], axis=-1)
        partial_stack = (
            jnp.dot(
                spectra,
                inverse,
                precision=lax.Precision.HIGHEST,
                preferred_element_type=jnp.float32,
            )
            * factor
        )
        results.append(lax.psum(partial_stack, "win"))
    combined = jnp.concatenate(results, axis=0)
    own_stack = lax.dynamic_slice_in_dim(combined, lax.axis_index("win") * per_win, per_win, 0)
    return own_stack


def solution(mesh):
    in_specs = (P("chan", "win", None), P())
    out_specs = P("win", "chan", None)
    return jax.shard_map(
        on_device, mesh=mesh, in_specs=in_specs, out_specs=out_specs, check_vma=False
    )
```

profile of v0, /device:TPU:0, one launch (start us, length us, event | category | flops | bytes accessed | tf_op | source)
XLA Modules:
  0.0 297.5 jit_solution(8172527145288458661)
XLA Ops:
  6.5 0.9 reshape.182
  7.5 0.2 convert_reduce_fusion
  7.6 1.8 multiply_reduce_fusion.16
  9.4 0.2 multiply_convert_fusion
  9.6 0.1 select_reduce_fusion
  9.7 0.5 convolution_convert_fusion.1
  10.2 0.8 copy.19
  11.1 0.1 pad.18
  11.2 1.3 reshape.185
  12.5 5.9 %fusion.34 = (f32[512,513]{0,1:T(8,128)}, f32[512,513]{0,1:T(8,128)}, f32[512,513]{0,1:T(8,128)}) fusion(pred[512]{0:T(512)(128)(4,1)S(1)} %iota_compare_fusion.2, f32[513]{0:T(1024)S(1)} %fusion.75), kind=kLoop, calls=%fused_computation.70 | loop fusion | flops 4990464 | bytes 3154436 | tf_op jit(solution)/shard_map/jit(_where)/select_n | solution.py:30
  18.4 8.4 %negate_select_fusion.2 = (f32[1024,512]{1,0:T(8,128)S(1)}, f32[1024,512]{1,0:T(8,128)S(1)}) fusion(f32[1024]{0:T(1024)S(1)} %fusion.73, pred[512]{0:T(512)(128)(4,1)S(1)} %iota_compare_fusion.2), kind=kLoop, calls=%fused_computation.34 | loop fusion | flops 8388608 | bytes 4198912 | tf_op jit(solution)/shard_map/jit(_where)/select_n | solution.py:24
  26.9 1.3 copy-done
  28.2 3.6 %fusion.8 = f32[8,120,1024]{2,1,0:T(8,128)S(1)} fusion(bf16[8,120,512]{2,1,0:T(8,128)(2,1)S(1)} %reshape.185, f32[1024,512]{1,0:T(8,128)S(1)} %get-tuple-element.53, f32[1024,512]{1,0:T(8,128)S(1)} %get-tuple-element.52), kind=kOutput, calls=%fused_computation.33 | convolution fusion | flops 6040322048 | bytes 9109504 | tf_op jit(solution)/shard_map/dot_general | solution.py:54
  31.8 2.3 fusion.97
  34.1 49.1 %all-gather.2.cloned.1.call-done = bf16[32,8,7500]{2,1,0:T(8,128)(2,1)} async-done(((bf16[4,8,7500]{2,1,0:T(8,128)(2,1)}), bf16[32,8,7500]{2,1,0:T(8,128)(2,1)}) %all-gather.2.cloned.1.call-update) | async-done | bytes 3840016 | tf_op jit(solution)/shard_map/all_gather | solution.py:76
  83.2 3.3 %convolution_convert_fusion = bf16[32,8,7500]{2,0,1:T(8,128)(2,1)S(1)} fusion(bf16[32,8,7500]{2,1,0:T(8,128)(2,1)} %all-gather.2.cloned.1.call-done, s32[32]{0:T(128)S(1)} %multiply_add_fusion), kind=kOutput, calls=%fused_computation.16 | convolution fusion | flops 124801024 | bytes 7680128 | tf_op jit(solution)/shard_map/sj,jwt->swt/dot_general | solution.py:79
  86.5 0.3 fusion.98
  86.8 0.1 pad.17
  86.9 0.1 fusion.101
  87.1 0.3 pad_maximum_fusion.1
  87.3 1.3 copy-done.1
  88.6 8.1 %fusion.19 = f32[8,120,1024]{2,1,0:T(8,128)S(1)} fusion(bf16[8,120,1024]{2,0,1:T(8,128)(2,1)S(1)} %bitcast.35, f32[1024,512]{1,0:T(8,128)S(1)} %get-tuple-element.52, f32[1024,512]{1,0:T(8,128)S(1)} %copy-done.1), kind=kOutput, calls=%fused_computation.48 | convolution fusion | flops 12080644096 | bytes 10092544 | tf_op jit(solution)/shard_map/dot_general | solution.py:91
  96.7 2.3 fusion.93
  99.0 0.1 pad.19
  99.1 0.1 fusion.99
  99.3 0.3 pad_maximum_fusion.2
  99.6 8.3 %fusion.17 = f32[8,120,1024]{2,1,0:T(8,128)S(1)} fusion(bf16[8,120,1024]{2,0,1:T(8,128)(2,1)S(1)} %bitcast.36, f32[1024,512]{1,0:T(8,128)S(1)} %get-tuple-element.52, f32[1024,512]{1,0:T(8,128)S(1)} %copy-done.1), kind=kOutput, calls=%fused_computation.46 | convolution fusion | flops 12080644096 | bytes 10092544 | tf_op jit(solution)/shard_map/dot_general | solution.py:91
  107.9 2.4 fusion.94
  110.3 0.1 pad.20
  110.4 0.1 fusion.100
  110.5 0.3 pad_maximum_fusion.3
  110.8 8.6 %fusion.15 = f32[8,120,1024]{2,1,0:T(8,128)S(1)} fusion(bf16[8,120,1024]{2,0,1:T(8,128)(2,1)S(1)} %bitcast.37, f32[1024,512]{1,0:T(8,128)S(1)} %get-tuple-element.52, f32[1024,512]{1,0:T(8,128)S(1)} %copy-done.1), kind=kOutput, calls=%fused_computation.44 | convolution fusion | flops 12080644096 | bytes 10092544 | tf_op jit(solution)/shard_map/dot_general | solution.py:91
  119.4 2.4 fusion.95
  121.8 0.1 pad.21
  121.8 0.1 fusion.102
  122.0 0.3 pad_maximum_fusion.4
  122.3 8.1 %fusion.13 = f32[8,120,1024]{2,1,0:T(8,128)S(1)} fusion(bf16[8,120,1024]{2,0,1:T(8,128)(2,1)S(1)} %bitcast.34, f32[1024,512]{1,0:T(8,128)S(1)} %get-tuple-element.52, f32[1024,512]{1,0:T(8,128)S(1)} %copy-done.1), kind=kOutput, calls=%fused_computation.42 | convolution fusion | flops 12080644096 | bytes 10092544 | tf_op jit(solution)/shard_map/dot_general | solution.py:91
  130.4 2.4 fusion.96
  132.9 1.1 copy-done.3
  133.9 0.6 copy-done.4
  134.5 103.1 %multiply_reduce_fusion.3 = (f32[8,8,512]{2,1,0:T(8,128)}, f32[8,8,512]{2,1,0:T(8,128)S(1)}, f32[8,8,512]{2,1,0:T(8,128)}, f32[8,8,512]{2,1,0:T(8,128)}, f32[8,8...) fusion(f32[8,120,512]{2,1,0:T(8,128)} %get-tuple-element.34, ...), kind=kLoop, calls=%fused_computation.3 | loop fusion | flops 125304832 | bytes 21757952 | tf_op jit(solution)/shard_map/reduce_sum | solution.py:96
  237.6 1.0 sub.34
  238.8 5.9 %convolution_multiply_fusion = f32[8,8,513]{2,1,0:T(8,128)} fusion(f32[512,513]{0,1:T(8,128)} %get-tuple-element.51, f32[512,513]{0,1:T(8,128)} %get-tuple-element.50, f32[512,513]{0,1:T(8,128)} %get-tuple-element.49, f32[8,8,512]{2,1,0:T(8,128)S(1)} %sub.34, f32[8,8,512]{2,1,0:T(8,128)} %get-tuple-element.9, f32[8,8,512]{2,1,0:T(8,128)} %get-tuple-element.5), kind=kOutput, calls=%fused_computation.55 | convolution fusion | flops 607752768 | bytes 3676416 | tf_op jit(solution)/shard_map/dot_general | solution.py:102
  244.8 3.8 %convolution_multiply_fusion.1 = f32[8,8,513]{2,1,0:T(8,128)} fusion(f32[512,513]{0,1:T(8,128)S(1)} %copy-done.8, f32[512,513]{0,1:T(8,128)S(1)} %copy-done.7, f32[512,513]{0,1:T(8,128)S(1)} %copy-done.6, f32[8,8,512]{2,1,0:T(8,128)S(1)} %sub.33, f32[8,8,512]{2,1,0:T(8,128)S(1)} %copy-done.13, f32[8,8,512]{2,1,0:T(8,128)S(1)} %copy-done.14), kind=kOutput, calls=%fused_computation.56 | convolution fusion | flops 607752768 | bytes 3676416 | tf_op jit(solution)/shard_map/dot_general | solution.py:102
  248.6 3.8 %convolution_multiply_fusion.2 = f32[8,8,513]{2,1,0:T(8,128)} fusion(f32[512,513]{0,1:T(8,128)S(1)} %copy-done.8, f32[512,513]{0,1:T(8,128)S(1)} %copy-done.7, f32[512,513]{0,1:T(8,128)S(1)} %copy-done.6, f32[8,8,512]{2,1,0:T(8,128)S(1)} %sub.32, f32[8,8,512]{2,1,0:T(8,128)S(1)} %copy-done.11, f32[8,8,512]{2,1,0:T(8,128)S(1)} %copy-done.12), kind=kOutput, calls=%fused_computation.57 | convolution fusion | flops 607752768 | bytes 3676416 | tf_op jit(solution)/shard_map/dot_general | solution.py:102
  252.4 3.8 %convolution_multiply_fusion.3 = f32[8,8,513]{2,1,0:T(8,128)} fusion(f32[512,513]{0,1:T(8,128)S(1)} %copy-done.8, f32[512,513]{0,1:T(8,128)S(1)} %copy-done.7, f32[512,513]{0,1:T(8,128)S(1)} %copy-done.6, f32[8,8,512]{2,1,0:T(8,128)S(1)} %sub.31, f32[8,8,512]{2,1,0:T(8,128)S(1)} %copy-done.9, f32[8,8,512]{2,1,0:T(8,128)S(1)} %copy-done.10), kind=kOutput, calls=%fused_computation.58 | convolution fusion | flops 607752768 | bytes 3676416 | tf_op jit(solution)/shard_map/dot_general | solution.py:102
  256.2 32.7 %all-reduce.8.cloned.1.call-done = (f32[8,8,513]{2,1,0:T(8,128)}, f32[8,8,513]{2,1,0:T(8,128)}, f32[8,8,513]{2,1,0:T(8,128)}, f32[8,8,513]{2,1,0:T(8,128)}) async-done(((f32[8,8,513]{2,1,0:T(8,128)}, f32[8,8,513]{2,1,0:T(8,128)}, f32[8,8,513]{2,1,0:T(8,128)}, f32[8,8,513]{2,1,0:T(8,128)}), (f32[8,8,513]{2,1,0:T(8,128)}, f32[8,8,513]{2,1,0:T(8,128)}, f32[8,8,513]{2,1,0:T(8,128)}, ...) | async-done | bytes 525328 | tf_op jit(solution)/shard_map/psum | solution.py:110
  288.9 1.6 fusion.61
  (40 shorter events, 0.2 us)
Async XLA Ops:
  6.5 2.9 copy-start.5
  6.5 76.7 %all-gather.2.cloned.1.call-start = ((), (), s32[]{:S(2)}) async-start(), calls=%async_computation | async-start | bytes 4349952 | tf_op jit(solution)/shard_map/all_gather | solution.py:76
  11.1 277.8 %all-reduce.8.cloned.1.call-start = ((), (), s32[]{:S(2)}) async-start(), calls=%async_computation.1 | async-start | bytes 1310720 | tf_op jit(solution)/shard_map/psum | solution.py:110
  26.9 1.3 copy-start
  87.0 1.6 copy-start.1
  130.4 2.5 copy-start.2
  130.4 3.5 %copy-start.3 = (f32[8,120,512]{2,1,0:T(8,128)S(1)}, f32[8,120,512]{2,1,0:T(8,128)}, u32[]{:S(2)}) copy-start(f32[8,120,512]{2,1,0:T(8,128)} %get-tuple-element.36) | copy-start | bytes 5898244
  130.4 4.1 %copy-start.4 = (f32[8,120,512]{2,1,0:T(8,128)S(1)}, f32[8,120,512]{2,1,0:T(8,128)}, u32[]{:S(2)}) copy-start(f32[8,120,512]{2,1,0:T(8,128)} %get-tuple-element.27) | copy-start | bytes 5898244
  238.7 6.0 %copy-start.6 = (f32[512,513]{0,1:T(8,128)S(1)}, f32[512,513]{0,1:T(8,128)}, u32[]{:S(2)}) copy-start(f32[512,513]{0,1:T(8,128)} %get-tuple-element.49) | copy-start | bytes 3151876
  238.7 6.0 %copy-start.7 = (f32[512,513]{0,1:T(8,128)S(1)}, f32[512,513]{0,1:T(8,128)}, u32[]{:S(2)}) copy-start(f32[512,513]{0,1:T(8,128)} %get-tuple-element.50) | copy-start | bytes 3151876
  238.7 6.0 %copy-start.8 = (f32[512,513]{0,1:T(8,128)S(1)}, f32[512,513]{0,1:T(8,128)}, u32[]{:S(2)}) copy-start(f32[512,513]{0,1:T(8,128)} %get-tuple-element.51) | copy-start | bytes 3151876
  238.7 6.0 %copy-start.13 = (f32[8,8,512]{2,1,0:T(8,128)S(1)}, f32[8,8,512]{2,1,0:T(8,128)}, u32[]{:S(2)}) copy-start(f32[8,8,512]{2,1,0:T(8,128)} %get-tuple-element.11) | copy-start | bytes 393220
  238.8 6.0 %copy-start.14 = (f32[8,8,512]{2,1,0:T(8,128)S(1)}, f32[8,8,512]{2,1,0:T(8,128)}, u32[]{:S(2)}) copy-start(f32[8,8,512]{2,1,0:T(8,128)} %get-tuple-element.14) | copy-start | bytes 393220
  244.7 3.8 %copy-start.11 = (f32[8,8,512]{2,1,0:T(8,128)S(1)}, f32[8,8,512]{2,1,0:T(8,128)}, u32[]{:S(2)}) copy-start(f32[8,8,512]{2,1,0:T(8,128)} %get-tuple-element.15) | copy-start | bytes 393220
  244.7 3.8 %copy-start.12 = (f32[8,8,512]{2,1,0:T(8,128)S(1)}, f32[8,8,512]{2,1,0:T(8,128)}, u32[]{:S(2)}) copy-start(f32[8,8,512]{2,1,0:T(8,128)} %get-tuple-element.18) | copy-start | bytes 393220
  248.5 3.8 %copy-start.9 = (f32[8,8,512]{2,1,0:T(8,128)S(1)}, f32[8,8,512]{2,1,0:T(8,128)}, u32[]{:S(2)}) copy-start(f32[8,8,512]{2,1,0:T(8,128)} %get-tuple-element.7) | copy-start | bytes 393220
  248.5 3.8 %copy-start.10 = (f32[8,8,512]{2,1,0:T(8,128)S(1)}, f32[8,8,512]{2,1,0:T(8,128)}, u32[]{:S(2)}) copy-start(f32[8,8,512]{2,1,0:T(8,128)} %get-tuple-element.20) | copy-start | bytes 393220
Sparse Core Ops, SparseCore 0:
  11.2 71.9 all-gather.1
  256.3 32.5 all-reduce.7
where the time goes:
time: 301 us; the launch traced here: 298 us
  other arithmetic  124 us (41%)
  waiting for transfers between devices  81.8 us (27%)
  matrix products  57.8 us (19%)
  local copies, waits for them, and re-layouts  20.4 us (7%)
  between operations  14 us (5%)
    reduce_sum x1, other arithmetic, on_device(): both_real = jnp.sum(probe_real * recv_real[None], axis=2)  103 us
    all_gather x1, waiting for transfers between devices, on_device(): gathered = lax.all_gather(picked, 'chan', axis=0, tiled=True)  49.1 us
    dot_general x4, matrix products, on_device(): jnp.dot(segments, forward, precision=lax.Precision.HIGHEST, preferred_ele...  33.1 us
    psum x1, waiting for transfers between devices, on_device(): results.append(lax.psum(partial_stack, 'win'))  32.7 us
    dot_general x4, matrix products, on_device(): jnp.dot(spectra, inverse, precision=lax.Precision.HIGHEST, preferred_elem...  17.3 us
    select_n x1, other arithmetic, make_tables(): sin_part = jnp.where(freqs == 0, alternate, -jnp.sin(phase))  8.44 us
    slice x3, local copies, waits for them, and re-layouts, on_device(): probe_real = probe_spec[:, :, :block_len][:, None]  7.11 us
  transfers between devices with their start and end apart: 2, of which 2 were waited for; matrix products, arithmetic and copies ran while one was open for 7% of the time, Pallas kernels for 0%

commit v1 on v0

v1 whole, which is shorter than its diff:
```python
import functools
import math

import jax
import jax.numpy as jnp
from jax import lax
from jax.experimental import pallas as pl
from jax.experimental.pallas import tpu as pltpu
from jax.sharding import PartitionSpec as P

MAX_LAG = 256
BLOCK = 128


def whiten(strain):
    mean_square = jnp.mean(strain * strain, axis=-1, keepdims=True)
    return (strain * lax.rsqrt(mean_square + 1e-06)).astype(jnp.bfloat16)


def correlate_kernel(factor, lag_blocks, order_ref, first_ref, second_ref, recv_ref, out_ref, probe_ref):
    channels = recv_ref.shape[0]
    depth = first_ref.shape[1]

    @pl.when(pl.program_id(0) == 0)
    def _():
        probe_ref[...] = jnp.zeros_like(probe_ref)

    probe_ref[:depth, :BLOCK] = first_ref[0]
    probe_ref[:depth, BLOCK:] = second_ref[0]
    row = lax.broadcasted_iota(jnp.int32, (BLOCK, BLOCK), 0)
    lane = lax.broadcasted_iota(jnp.int32, (BLOCK, BLOCK), 1)
    later = row + lane >= BLOCK - 1
    diagonal = row + lane == BLOCK - 1
    for channel in range(channels):
        products = jnp.dot(recv_ref[channel], probe_ref[...], preferred_element_type=jnp.float32)
        for half in range(2):
            columns = products[:, half * BLOCK : (half + 1) * BLOCK]
            parts = [columns[k * BLOCK : (k + 1) * BLOCK] for k in range(lag_blocks + 1)]
            for k in range(lag_blocks):
                mixed = jnp.where(later, parts[k], parts[k + 1])
                sheared = pltpu.roll(mixed, 0, 1, stride=1, stride_axis=0)
                total = jnp.sum(sheared, axis=0, keepdims=True)
                out_ref[half, channel : channel + 1, k * BLOCK : (k + 1) * BLOCK] = (
                    pltpu.roll(total, 1, 1) * factor
                )
            last = jnp.where(diagonal, parts[lag_blocks], 0.0)
            last = jnp.sum(jnp.sum(last, axis=0, keepdims=True), axis=1, keepdims=True)
            out_ref[half, channel : channel + 1, lag_blocks * BLOCK :] = last * factor


def correlate(gathered, receivers, order, factor):
    total, depth, _ = gathered.shape
    channels, rows, inner = receivers.shape
    lag_blocks = 2 * MAX_LAG // BLOCK
    lag_count = 2 * MAX_LAG + 1
    return pl.pallas_call(
        functools.partial(correlate_kernel, factor, lag_blocks),
        out_shape=jax.ShapeDtypeStruct((total, channels, lag_count), jnp.float32),
        grid_spec=pltpu.PrefetchScalarGridSpec(
            num_scalar_prefetch=1,
            grid=(total // 2,),
            in_specs=[
                pl.BlockSpec((1, depth, BLOCK), lambda p, order: (order[2 * p], 0, 0)),
                pl.BlockSpec((1, depth, BLOCK), lambda p, order: (order[2 * p + 1], 0, 0)),
                pl.BlockSpec((channels, rows, inner), lambda p, order: (0, 0, 0)),
            ],
            out_specs=pl.BlockSpec((2, channels, lag_count), lambda p, order: (p, 0, 0)),
            scratch_shapes=[pltpu.VMEM((inner, 2 * BLOCK), jnp.bfloat16)],
        ),
        compiler_params=pltpu.CompilerParams(vmem_limit_bytes=48 * 1024 * 1024),
    )(order, gathered, gathered, receivers)


def on_device(strain, sources):
    channels, windows, samples = strain.shape
    rounds, per_round = sources.shape
    total_sources = rounds * per_round
    lag_blocks = 2 * MAX_LAG // BLOCK
    ahead = MAX_LAG // BLOCK
    factor = 1.0 / math.sqrt(lax.axis_size("win") * windows * samples)
    blocks = -(-samples // BLOCK)
    while blocks * windows % 16:
        blocks += 1
    depth = blocks * windows
    inner = -(-depth // 256) * 256

    whitened = whiten(strain)
    padded = jnp.pad(whitened, ((0, 0), (0, 0), (0, blocks * BLOCK - samples)))
    pieces = padded.reshape(channels, windows, blocks, BLOCK)
    pieces = jnp.transpose(pieces, (0, 2, 1, 3)).reshape(channels, depth, BLOCK)

    flat_sources = sources.reshape(-1)
    per_shard = total_sources // lax.axis_size("chan")
    owner = flat_sources // channels
    position = jnp.arange(total_sources)
    earlier = (owner[None, :] == owner[:, None]) & (position[None, :] < position[:, None])
    rank = jnp.sum(earlier.astype(jnp.int32), axis=1)
    me = lax.axis_index("chan")
    mine = owner == me
    slot_pick = (mine[None, :] & (rank[None, :] == jnp.arange(per_shard)[:, None])).astype(jnp.int32)
    local_channel = jnp.sum(slot_pick * (flat_sources - me * channels)[None, :], axis=1)
    picked = jnp.concatenate(
        [lax.dynamic_slice_in_dim(pieces, local_channel[i], 1, 0) for i in range(per_shard)], axis=0
    )
    gathered = lax.all_gather(picked, "chan", axis=0, tiled=True)
    order = (owner * per_shard + rank).astype(jnp.int32)

    reverse = (jnp.arange(BLOCK)[:, None] + jnp.arange(BLOCK)[None, :] == BLOCK - 1).astype(jnp.bfloat16)
    flipped = lax.dot_general(
        pieces, reverse, (((2,), (1,)), ((), ())), preferred_element_type=jnp.float32
    ).astype(jnp.bfloat16)
    flipped = jnp.transpose(flipped, (0, 2, 1))
    front = (lag_blocks - ahead) * windows
    back = inner + lag_blocks * windows - front - depth
    flipped = jnp.pad(flipped, ((0, 0), (0, 0), (front, back)))
    receivers = jnp.concatenate(
        [
            flipped[:, :, (lag_blocks - k) * windows : (lag_blocks - k) * windows + inner]
            for k in range(lag_blocks + 1)
        ],
        axis=1,
    )
    partial_stack = correlate(gathered, receivers, order, factor)
    return lax.psum_scatter(partial_stack, "win", scatter_dimension=0, tiled=True)


def solution(mesh):
    in_specs = (P("chan", "win", None), P())
    out_specs = P("win", "chan", None)
    return jax.shard_map(
        on_device, mesh=mesh, in_specs=in_specs, out_specs=out_specs, check_vma=False
    )
```

time: 301 us -> 158 us (0.52); the launches traced: 298 us -> 158 us
  other arithmetic: 124 us -> 4.7 us
  matrix products: 57.8 us -> 0.41 us
  Pallas kernels: 0 us -> 34.8 us
  local copies, waits for them, and re-layouts: 20.4 us -> 8.49 us
  between operations: 14 us -> 21.1 us
  waiting for transfers between devices: 81.8 us -> 88.6 us
    reduce_sum x2 -> x1, other arithmetic: 103 us -> 0.12 us  [on_device(): jnp.sum(slot_pick * (flat_sources - me * channels)[None, :], axis=1)]
    dot_general x11 -> x1, matrix products: 57.8 us -> 0.41 us  [on_device(): lax.dot_general(pieces, reverse, (((2,), (1,)), ((), ())), preferred_elem...]
    pallas_call x0 -> x1, Pallas kernels: none -> 34.8 us  [correlate(): pl.pallas_call(functools.partial(correlate_kernel, factor, lag_blocks), o...]
    psum x1 -> x0, waiting for transfers between devices: 32.7 us -> none  [on_device(): results.append(lax.psum(partial_stack, 'win'))]
    reduce_scatter x0 -> x1, waiting for transfers between devices: none -> 20.9 us  [on_device(): lax.psum_scatter(partial_stack, 'win', scatter_dimension=0, tiled=True)]
    all_gather x1, waiting for transfers between devices: 49.1 us -> 67.6 us  [on_device(): gathered = lax.all_gather(picked, 'chan', axis=0, tiled=True)]
    select_n x4 -> x0, other arithmetic: 14.3 us -> none  [the longest x1 8.44 us: make_tables(): sin_part = jnp.where(freqs == 0, alternate, -jnp.sin(phase))]
    slice x10 -> x1, local copies, waits for them, and re-layouts: 12.7 us -> 0.67 us  [on_device(): local_channel[i]]
  transfers between devices with their start and end apart: 2 -> 2, of which waited for: 2 -> 2; matrix products, arithmetic and copies ran while one was open for 7% -> 2% of each run, Pallas kernels for 0% -> 0%
where the time goes in v1:
time: 158 us
  waiting for transfers between devices  88.6 us (56%)
  Pallas kernels  34.8 us (22%)
  between operations  21.1 us (13%)
  local copies, waits for them, and re-layouts  8.49 us (5%)
  other arithmetic  4.7 us (3%)
    all_gather x1, waiting for transfers between devices, on_device(): gathered = lax.all_gather(picked, 'chan', axis=0, tiled=True)  67.6 us
    pallas_call x1, Pallas kernels, correlate(): pl.pallas_call(functools.partial(correlate_kernel, factor, lag_blocks), o...  34.8 us
    reduce_scatter x1, waiting for transfers between devices, on_device(): lax.psum_scatter(partial_stack, 'win', scatter_dimension=0, tiled=True)  20.9 us
    unnamed x8, local copies, waits for them, and re-layouts  5.92 us
  transfers between devices with their start and end apart: 2, of which 2 were waited for; matrix products, arithmetic and copies ran while one was open for 2% of the time, Pallas kernels for 0%

profile of v1, /device:TPU:0, one launch (start us, length us, event | category | flops | bytes accessed | tf_op | source)
XLA Modules:
  0.0 158.1 jit_solution(10001907391466807116)
XLA Ops:
  6.5 0.0 all-gather.2.cloned.1.call-start
  6.5 0.8 reshape.89
  7.3 0.2 convert_reduce_fusion
  7.5 0.1 select_reduce_fusion
  7.6 0.7 fusion.11
  13.4 1.8 %multiply_reduce_fusion = f32[8,8]{1,0:T(8,128)S(1)} fusion(f32[8,8,7500]{2,1,0:T(8,128)} %param.2), kind=kLoop, calls=%fused_computation.1 | loop fusion | flops 959936 | bytes 1920256 | tf_op jit(solution)/shard_map/reduce_sum | solution.py:16
  15.1 1.7 %multiply_convert_fusion = bf16[8,8,7500]{2,1,0:T(8,128)(2,1)S(1)} fusion(f32[8,8,7500]{2,1,0:T(8,128)} %param.2, f32[8,8]{1,0:T(8,128)S(1)} %add_rsqrt_fusion), kind=kLoop, calls=%fused_computation | loop fusion | flops 960000 | bytes 2880256 | tf_op jit(solution)/shard_map/convert_element_type | solution.py:17
  16.9 0.1 pad_bitcast_fusion
  19.5 0.9 pad_maximum_fusion
  20.4 0.0 all-gather.2.cloned.1.call-update
  20.4 0.0 reduce-scatter.2.cloned.1.call-start
  20.5 0.4 convolution_convert_fusion
  20.9 0.5 copy.6
  21.4 0.4 fusion
  21.9 0.5 fusion.1
  22.3 0.1 fusion.2
  22.5 0.5 fusion.3
  23.0 0.5 fusion.4.recv_ref
  23.5 0.0 copy-start.1
  23.5 2.3 %copy-done.1 = bf16[8,640,512]{2,1,0:T(8,128)(2,1)} copy-done((bf16[8,640,512]{2,1,0:T(8,128)(2,1)}, bf16[8,640,512]{2,1,0:T(8,128)(2,1)S(1)}, u32[]{:S(2)}) %copy-start.1) | copy-done | bytes 5242904
  25.8 67.6 %all-gather.2.cloned.1.call-done.first_ref.second_ref = bf16[32,480,128]{2,1,0:T(8,128)(2,1)} async-done(((bf16[4,480,128]{2,1,0:T(8,128)(2,1)}), bf16[32,480,128]{2,1,0:T(8,128)(2,1)}) %all-gather.2.cloned.1.call-update) | async-done | bytes 3932176 | tf_op jit(solution)/shard_map/all_gather | solution.py:105
  93.4 0.0 copy-start
  93.4 2.1 %copy-done = bf16[32,480,128]{2,1,0:T(8,128)(2,1)S(1)} copy-done((bf16[32,480,128]{2,1,0:T(8,128)(2,1)S(1)}, bf16[32,480,128]{2,1,0:T(8,128)(2,1)}, u32[]{:S(2)}) %copy-start) | copy-done | bytes 3932184
  95.5 34.8 %shard_map.28 = f32[32,8,513]{2,1,0:T(8,128)} custom-call(s32[32]{0:T(128)S(1)} %multiply_add_fusion.order_ref, bf16[32,480,128]{2,1,0:T(8,128)(2,1)S(1)} %copy-done, bf16[32,480,128]{2,1,0:T(8,128)(2,1)S(1)} %copy-done, bf16[8,640,512]{2,1,0:T(8,128)(2,1)} %copy-done.1), custom_call_target="tpu_custom_call" | custom-call | tf_op jit(solution)/shard_map/pallas_call | solution.py:56
  130.3 0.0 reduce-scatter.2.cloned.1.call-update
  130.3 20.9 %reduce-scatter.2.cloned.1.call-done = f32[8,8,513]{2,1,0:T(8,128)} async-done(((f32[32,8,513]{2,1,0:T(8,128)}), f32[8,8,513]{2,1,0:T(8,128)}) %reduce-scatter.2.cloned.1.call-update) | async-done | bytes 131344 | tf_op jit(solution)/shard_map/reduce_scatter | solution.py:124
  (5 shorter events, 0.1 us)
Async XLA Ops:
  6.5 86.8 %all-gather.2.cloned.1.call-start = ((), (), s32[]{:S(2)}) async-start(), calls=%async_computation.1 | async-start | bytes 4423680 | tf_op jit(solution)/shard_map/all_gather | solution.py:105
  20.4 130.8 %reduce-scatter.2.cloned.1.call-start = ((), (), s32[]{:S(2)}) async-start(), calls=%async_computation.2 | async-start | bytes 819200 | tf_op jit(solution)/shard_map/reduce_scatter | solution.py:124
  23.5 2.3 %copy-start.1 = (bf16[8,640,512]{2,1,0:T(8,128)(2,1)}, bf16[8,640,512]{2,1,0:T(8,128)(2,1)S(1)}, u32[]{:S(2)}) copy-start(bf16[8,640,512]{2,1,0:T(8,128)(2,1)S(1)} %fusion.4.recv_ref) | copy-start | bytes 15728644
  93.4 2.1 %copy-start = (bf16[32,480,128]{2,1,0:T(8,128)(2,1)S(1)}, bf16[32,480,128]{2,1,0:T(8,128)(2,1)}, u32[]{:S(2)}) copy-start(bf16[32,480,128]{2,1,0:T(8,128)(2,1)} %all-gather.2.cloned.1.call-done.first_ref.second_ref) | copy-start | bytes 11796484
Sparse Core Ops, SparseCore 0:
  20.5 72.7 all-gather.1
  130.4 20.7 reduce-scatter.1

commit v2 on v1

v2 whole, which is shorter than its diff:
```python
import functools
import math

import jax
import jax.numpy as jnp
from jax import lax
from jax.experimental import pallas as pl
from jax.experimental.pallas import tpu as pltpu
from jax.sharding import PartitionSpec as P

MAX_LAG = 256
BLOCK = 128


def whiten(strain):
    mean_square = jnp.mean(strain * strain, axis=-1, keepdims=True)
    return (strain * lax.rsqrt(mean_square + 1e-06)).astype(jnp.bfloat16)


def ring_position(index, size):
    odd = lax.rem(index, 2)
    half = index // 2
    return (1 - odd) * half + odd * (size - 1 - half)


def ring_index(position, size):
    back = position // (size // 2)
    return (1 - back) * 2 * position + back * (2 * (size - 1 - position) + 1)


def kernel(
    sizes, factor, picked_ref, recv_ref, order_ref, out_ref,
    held_ref, probe_ref, partial_ref, send_ref, land_ref,
    send_sem, recv_sem, stack_send_sem, stack_recv_sem,
):
    chan_size, win_size, lag_blocks = sizes
    channels = recv_ref.shape[0]
    ways, _, count, depth, _ = held_ref.shape
    per_shard = ways * count
    here = ring_position(lax.axis_index("chan"), chan_size)
    win = lax.axis_index("win")
    right = ring_index(lax.rem(here + 1, chan_size), chan_size)
    left = ring_index(lax.rem(here + chan_size - 1, chan_size), chan_size)
    targets = [right, left]

    barrier = pltpu.get_barrier_semaphore()
    for chan in targets:
        pl.semaphore_signal(barrier, inc=1, device_id={"chan": chan}, device_id_type=pl.DeviceIdType.MESH)
    for step in range(1, win_size):
        peer = lax.rem(win + step, win_size)
        pl.semaphore_signal(barrier, inc=1, device_id={"win": peer}, device_id_type=pl.DeviceIdType.MESH)
    for way in range(ways):
        held_ref[way, 0] = picked_ref[way * count : (way + 1) * count]
    probe_ref[...] = jnp.zeros_like(probe_ref)
    pl.semaphore_wait(barrier, len(targets) + win_size - 1)

    row = lax.broadcasted_iota(jnp.int32, (BLOCK, BLOCK), 0)
    lane = lax.broadcasted_iota(jnp.int32, (BLOCK, BLOCK), 1)
    later = row + lane >= BLOCK - 1
    diagonal = row + lane == BLOCK - 1

    def hop(way, step, item):
        return pltpu.make_async_remote_copy(
            src_ref=held_ref.at[way, step, item],
            dst_ref=held_ref.at[way, step + 1, item],
            send_sem=send_sem.at[way, step, item],
            recv_sem=recv_sem.at[way, step, item],
            device_id={"chan": targets[way]},
            device_id_type=pl.DeviceIdType.MESH,
        )

    def work(way, step):
        origin = here - step if way == 0 else here + step
        origin = ring_index(lax.rem(origin + chan_size, chan_size), chan_size)
        for item in range(count):
            probe_ref[way, :depth, item * BLOCK : (item + 1) * BLOCK] = held_ref[way, step, item]
        for channel in range(channels):
            products = jnp.dot(recv_ref[channel], probe_ref[way], preferred_element_type=jnp.float32)
            for item in range(count):
                columns = products[:, item * BLOCK : (item + 1) * BLOCK]
                parts = [columns[k * BLOCK : (k + 1) * BLOCK] for k in range(lag_blocks + 1)]
                totals = []
                for k in range(lag_blocks):
                    mixed = jnp.where(later, parts[k], parts[k + 1])
                    sheared = pltpu.roll(mixed, 0, 1, stride=1, stride_axis=0)
                    total = jnp.sum(sheared, axis=0, keepdims=True)
                    totals.append(pltpu.roll(total, 1, 1) * factor)
                last = jnp.where(diagonal, parts[lag_blocks], 0.0)
                last = jnp.sum(jnp.sum(last, axis=0, keepdims=True), axis=1, keepdims=True)
                totals.append(jnp.broadcast_to(last * factor, (1, BLOCK)))
                place = origin * per_shard + way * count + item
                partial_ref[place, channel : channel + 1, :] = jnp.concatenate(totals, axis=1)

    for way in range(ways):
        for item in range(count):
            hop(way, 0, item).start()

    slots = max(ways, count)

    def body(step, carry):
        for slot in range(slots):
            if slot < count:
                for way in range(ways):
                    hop(way, step - 1, slot).wait_recv()

                    @pl.when(step < chan_size - 1)
                    def _():
                        hop(way, step, slot).start()

            if slot < ways:
                work(slot, step - 1)
        return carry

    lax.fori_loop(1, chan_size, body, 0)
    for way in range(ways):
        work(way, chan_size - 1)
    for step in range(chan_size - 1):
        for way in range(ways):
            for item in range(count):
                hop(way, step, item).wait_send()

    per_win = out_ref.shape[0]
    for dest in range(win_size):
        for item in range(per_win):
            send_ref[dest, item] = partial_ref[order_ref[dest * per_win + item]]

    def stack_copy(step):
        peer = lax.rem(win + step, win_size)
        return pltpu.make_async_remote_copy(
            src_ref=send_ref.at[peer],
            dst_ref=land_ref.at[step - 1],
            send_sem=stack_send_sem.at[step - 1],
            recv_sem=stack_recv_sem.at[step - 1],
            device_id={"win": peer},
            device_id_type=pl.DeviceIdType.MESH,
        )

    for step in range(1, win_size):
        stack_copy(step).start()
    for step in range(1, win_size):
        stack_copy(step).wait_recv()
    total = send_ref[win]
    for step in range(1, win_size):
        total = total + land_ref[step - 1]
    out_ref[...] = total[:, :, : out_ref.shape[2]]
    for step in range(1, win_size):
        stack_copy(step).wait_send()


def correlate(picked, receivers, order, factor):
    per_shard, depth, _ = picked.shape
    channels, rows, inner = receivers.shape
    total = order.shape[0]
    chan_size, win_size = lax.axis_size("chan"), lax.axis_size("win")
    lag_blocks = 2 * MAX_LAG // BLOCK
    lag_count = 2 * MAX_LAG + 1
    lanes = (lag_blocks + 1) * BLOCK
    per_win = total // win_size
    ways = 2 if per_shard % 2 == 0 else 1
    count = per_shard // ways
    return pl.pallas_call(
        functools.partial(kernel, (chan_size, win_size, lag_blocks), factor),
        out_shape=jax.ShapeDtypeStruct((per_win, channels, lag_count), jnp.float32),
        in_specs=[
            pl.BlockSpec(memory_space=pltpu.VMEM),
            pl.BlockSpec(memory_space=pltpu.VMEM),
            pl.BlockSpec(memory_space=pltpu.SMEM),
        ],
        out_specs=pl.BlockSpec(memory_space=pltpu.VMEM),
        scratch_shapes=[
            pltpu.VMEM((ways, chan_size, count, depth, BLOCK), jnp.bfloat16),
            pltpu.VMEM((ways, inner, count * BLOCK), jnp.bfloat16),
            pltpu.VMEM((total, channels, lanes), jnp.float32),
            pltpu.VMEM((win_size, per_win, channels, lanes), jnp.float32),
            pltpu.VMEM((win_size - 1, per_win, channels, lanes), jnp.float32),
            pltpu.SemaphoreType.DMA((ways, chan_size - 1, count)),
            pltpu.SemaphoreType.DMA((ways, chan_size - 1, count)),
            pltpu.SemaphoreType.DMA((win_size - 1,)),
            pltpu.SemaphoreType.DMA((win_size - 1,)),
        ],
        compiler_params=pltpu.CompilerParams(
            vmem_limit_bytes=48 * 1024 * 1024, collective_id=0, has_side_effects=True
        ),
    )(picked, receivers, order)


def on_device(strain, sources):
    channels, windows, samples = strain.shape
    rounds, per_round = sources.shape
    total_sources = rounds * per_round
    lag_blocks = 2 * MAX_LAG // BLOCK
    ahead = MAX_LAG // BLOCK
    factor = 1.0 / math.sqrt(lax.axis_size("win") * windows * samples)
    blocks = -(-samples // BLOCK)
    while blocks * windows % 16:
        blocks += 1
    depth = blocks * windows
    inner = -(-depth // 256) * 256

    whitened = whiten(strain)
    padded = jnp.pad(whitened, ((0, 0), (0, 0), (0, blocks * BLOCK - samples)))
    pieces = padded.reshape(channels, windows, blocks, BLOCK)
    pieces = jnp.transpose(pieces, (0, 2, 1, 3)).reshape(channels, depth, BLOCK)

    flat_sources = sources.reshape(-1)
    per_shard = total_sources // lax.axis_size("chan")
    owner = flat_sources // channels
    position = jnp.arange(total_sources)
    earlier = (owner[None, :] == owner[:, None]) & (position[None, :] < position[:, None])
    rank = jnp.sum(earlier.astype(jnp.int32), axis=1)
    me = lax.axis_index("chan")
    mine = owner == me
    slot_pick = (mine[None, :] & (rank[None, :] == jnp.arange(per_shard)[:, None])).astype(jnp.int32)
    local_channel = jnp.sum(slot_pick * (flat_sources - me * channels)[None, :], axis=1)
    picked = jnp.concatenate(
        [lax.dynamic_slice_in_dim(pieces, local_channel[i], 1, 0) for i in range(per_shard)], axis=0
    )
    order = (owner * per_shard + rank).astype(jnp.int32)

    reverse = (jnp.arange(BLOCK)[:, None] + jnp.arange(BLOCK)[None, :] == BLOCK - 1).astype(jnp.bfloat16)
    flipped = lax.dot_general(
        pieces, reverse, (((2,), (1,)), ((), ())), preferred_element_type=jnp.float32
    ).astype(jnp.bfloat16)
    flipped = jnp.transpose(flipped, (0, 2, 1))
    front = (lag_blocks - ahead) * windows
    back = inner + lag_blocks * windows - front - depth
    flipped = jnp.pad(flipped, ((0, 0), (0, 0), (front, back)))
    receivers = jnp.concatenate(
        [
            flipped[:, :, (lag_blocks - k) * windows : (lag_blocks - k) * windows + inner]
            for k in range(lag_blocks + 1)
        ],
        axis=1,
    )
    return correlate(picked, receivers, order, factor)


def solution(mesh):
    in_specs = (P("chan", "win", None), P())
    out_specs = P("win", "chan", None)
    return jax.shard_map(
        on_device, mesh=mesh, in_specs=in_specs, out_specs=out_specs, check_vma=False
    )
```

time: 158 us -> 73.3 us (0.46)
  waiting for transfers between devices: 88.6 us -> 0 us
  Pallas kernels: 34.8 us -> 55.7 us
  between operations: 21.1 us -> 7.69 us
  local copies, waits for them, and re-layouts: 8.49 us -> 4.82 us
    all_gather x1 -> x0, waiting for transfers between devices: 67.6 us -> none  [on_device(): gathered = lax.all_gather(picked, 'chan', axis=0, tiled=True)]
    pallas_call x1, Pallas kernels: 34.8 us -> 55.7 us  [correlate(): pl.pallas_call(functools.partial(kernel, (chan_size, win_size, lag_blocks...]
    reduce_scatter x1 -> x0, waiting for transfers between devices: 20.9 us -> none  [on_device(): lax.psum_scatter(partial_stack, 'win', scatter_dimension=0, tiled=True)]
    unnamed x8 -> x5, local copies, waits for them, and re-layouts: 5.92 us -> 2.23 us
  transfers between devices with their start and end apart: 2 -> 0, of which waited for: 2 -> 0; matrix products, arithmetic and copies ran while one was open for 2% -> 0% of each run, Pallas kernels for 0% -> 0%
where the time goes in v2:
time: 73.3 us; the launch traced here: 72.6 us
  Pallas kernels  55.7 us (76%)
  between operations  7.69 us (10%)
  local copies, waits for them, and re-layouts  4.82 us (7%)
  other arithmetic  3.88 us (5%)
    pallas_call x1, Pallas kernels, correlate(): pl.pallas_call(functools.partial(kernel, (chan_size, win_size, lag_blocks...  55.7 us
    unnamed x5, local copies, waits for them, and re-layouts  2.23 us
    reduce_sum x1, other arithmetic, whiten(): mean_square = jnp.mean(strain * strain, axis=-1, keepdims=True)  1.77 us
    convert_element_type x1, other arithmetic, whiten(): return (strain * lax.rsqrt(mean_square + 1e-06)).astype(jnp.bfloat16)  1.72 us

profile of v2, /device:TPU:0, one launch (start us, length us, event | category | flops | bytes accessed | tf_op | source)
XLA Modules:
  0.0 72.6 jit_solution(4045367382485428260)
XLA Ops:
  0.0 0.8 %reshape.91 = s32[32]{0:T(128)S(1)} reshape(s32[4,8]{1,0:T(4,128)} %param.3) | data formatting | bytes 256 | tf_op jit(solution)/shard_map/reshape | solution.py:205
  0.8 0.2 convert_reduce_fusion
  1.0 0.1 select_reduce_fusion
  1.1 0.7 fusion.11
  9.4 1.8 %multiply_reduce_fusion = f32[8,8]{1,0:T(8,128)S(1)} fusion(f32[8,8,7500]{2,1,0:T(8,128)} %param.2), kind=kLoop, calls=%fused_computation.1 | loop fusion | flops 959936 | bytes 1920256 | tf_op jit(solution)/shard_map/reduce_sum | solution.py:16
  11.1 1.7 %multiply_convert_fusion = bf16[8,8,7500]{2,1,0:T(8,128)(2,1)S(1)} fusion(f32[8,8,7500]{2,1,0:T(8,128)} %param.2, f32[8,8]{1,0:T(8,128)S(1)} %add_rsqrt_fusion), kind=kLoop, calls=%fused_computation | loop fusion | flops 960000 | bytes 2880256 | tf_op jit(solution)/shard_map/convert_element_type | solution.py:17
  12.9 0.4 convolution_convert_fusion
  13.3 0.1 pad_bitcast_fusion
  13.4 0.1 pad_maximum_fusion.picked_ref
  13.5 0.5 copy.5
  14.0 0.4 fusion
  14.5 0.5 fusion.1
  14.9 0.2 fusion.2
  15.1 0.5 fusion.3
  15.6 0.5 fusion.4.recv_ref
  16.1 55.7 %shard_map.28 = f32[8,8,513]{2,1,0:T(8,128)S(1)} custom-call(bf16[4,480,128]{2,1,0:T(8,128)(2,1)S(1)} %pad_maximum_fusion.picked_ref, bf16[8,640,512]{2,1,0:T(8,128)(2,1)S(1)} %fusion.4.recv_ref, s32[32]{0:T(128)S(1)} %multiply_add_fusion.order_ref), custom_call_target="tpu_custom_call" | custom-call | tf_op jit(solution)/shard_map/pallas_call | solution.py:161
  71.9 0.7 copy.11
  (5 shorter events, 0.1 us)

commit v3 on v2

--- a/solution.py
+++ b/solution.py
@@ -29,11 +29,11 @@
 
 
 def kernel(
-    sizes, factor, picked_ref, recv_ref, order_ref, out_ref,
-    held_ref, probe_ref, partial_ref, send_ref, land_ref,
+    sizes, factor, pieces_ref, local_ref, order_ref, out_ref,
+    recv_ref, wide_ref, held_ref, probe_ref, partial_ref, send_ref, land_ref,
     send_sem, recv_sem, stack_send_sem, stack_recv_sem,
 ):
-    chan_size, win_size, lag_blocks = sizes
+    chan_size, win_size, lag_blocks, windows, front = sizes
     channels = recv_ref.shape[0]
     ways, _, count, depth, _ = held_ref.shape
     per_shard = ways * count
@@ -50,7 +50,8 @@
         peer = lax.rem(win + step, win_size)
         pl.semaphore_signal(barrier, inc=1, device_id={"win": peer}, device_id_type=pl.DeviceIdType.MESH)
     for way in range(ways):
-        held_ref[way, 0] = picked_ref[way * count : (way + 1) * count]
+        for item in range(count):
+            held_ref[way, 0, item] = pieces_ref[local_ref[way * count + item]]
     probe_ref[...] = jnp.zeros_like(probe_ref)
     pl.semaphore_wait(barrier, len(targets) + win_size - 1)
 
@@ -95,6 +96,20 @@
         for item in range(count):
             hop(way, 0, item).start()
 
+    reverse = jnp.where(diagonal, 1.0, 0.0).astype(jnp.bfloat16)
+    inner = recv_ref.shape[2]
+    reach = wide_ref.shape[1]
+    wide_ref[...] = jnp.zeros_like(wide_ref)
+    for channel in range(channels):
+        wide_ref[channel % 2, front : front + depth, :] = pieces_ref[channel]
+        flipped = lax.dot_general(
+            reverse, wide_ref[channel % 2], (((1,), (1,)), ((), ())), preferred_element_type=jnp.float32
+        )
+        for k in range(lag_blocks + 1):
+            shift = (lag_blocks - k) * windows
+            moved = pltpu.roll(flipped, reach - shift, 1) if shift else flipped
+            recv_ref[channel, k * BLOCK : (k + 1) * BLOCK, :] = moved[:, :inner].astype(jnp.bfloat16)
+
     slots = max(ways, count)
 
     def body(step, carry):
@@ -147,27 +162,32 @@
         stack_copy(step).wait_send()
 
 
-def correlate(picked, receivers, order, factor):
-    per_shard, depth, _ = picked.shape
-    channels, rows, inner = receivers.shape
+def correlate(pieces, local_channel, order, windows, factor):
+    channels, depth, _ = pieces.shape
+    per_shard = local_channel.shape[0]
     total = order.shape[0]
     chan_size, win_size = lax.axis_size("chan"), lax.axis_size("win")
     lag_blocks = 2 * MAX_LAG // BLOCK
     lag_count = 2 * MAX_LAG + 1
+    front = (lag_blocks - MAX_LAG // BLOCK) * windows
+    inner = -(-depth // 256) * 256
+    reach = -(-(inner + lag_blocks * windows) // BLOCK) * BLOCK
     lanes = (lag_blocks + 1) * BLOCK
     per_win = total // win_size
     ways = 2 if per_shard % 2 == 0 else 1
     count = per_shard // ways
     return pl.pallas_call(
-        functools.partial(kernel, (chan_size, win_size, lag_blocks), factor),
+        functools.partial(kernel, (chan_size, win_size, lag_blocks, windows, front), factor),
         out_shape=jax.ShapeDtypeStruct((per_win, channels, lag_count), jnp.float32),
         in_specs=[
             pl.BlockSpec(memory_space=pltpu.VMEM),
-            pl.BlockSpec(memory_space=pltpu.VMEM),
+            pl.BlockSpec(memory_space=pltpu.SMEM),
             pl.BlockSpec(memory_space=pltpu.SMEM),
         ],
         out_specs=pl.BlockSpec(memory_space=pltpu.VMEM),
         scratch_shapes=[
+            pltpu.VMEM((channels, (lag_blocks + 1) * BLOCK, inner), jnp.bfloat16),
+            pltpu.VMEM((2, reach, BLOCK), jnp.bfloat16),
             pltpu.VMEM((ways, chan_size, count, depth, BLOCK), jnp.bfloat16),
             pltpu.VMEM((ways, inner, count * BLOCK), jnp.bfloat16),
             pltpu.VMEM((total, channels, lanes), jnp.float32),
@@ -181,21 +201,18 @@
         compiler_params=pltpu.CompilerParams(
             vmem_limit_bytes=48 * 1024 * 1024, collective_id=0, has_side_effects=True
         ),
-    )(picked, receivers, order)
+    )(pieces, local_channel, order)
 
 
 def on_device(strain, sources):
     channels, windows, samples = strain.shape
     rounds, per_round = sources.shape
     total_sources = rounds * per_round
-    lag_blocks = 2 * MAX_LAG // BLOCK
-    ahead = MAX_LAG // BLOCK
     factor = 1.0 / math.sqrt(lax.axis_size("win") * windows * samples)
     blocks = -(-samples // BLOCK)
     while blocks * windows % 16:
         blocks += 1
     depth = blocks * windows
-    inner = -(-depth // 256) * 256
 
     whitened = whiten(strain)
     padded = jnp.pad(whitened, ((0, 0), (0, 0), (0, blocks * BLOCK - samples)))
@@ -212,27 +229,9 @@
     mine = owner == me
     slot_pick = (mine[None, :] & (rank[None, :] == jnp.arange(per_shard)[:, None])).astype(jnp.int32)
     local_channel = jnp.sum(slot_pick * (flat_sources - me * channels)[None, :], axis=1)
-    picked = jnp.concatenate(
-        [lax.dynamic_slice_in_dim(pieces, local_channel[i], 1, 0) for i in range(per_shard)], axis=0
-    )
     order = (owner * per_shard + rank).astype(jnp.int32)
 
-    reverse = (jnp.arange(BLOCK)[:, None] + jnp.arange(BLOCK)[None, :] == BLOCK - 1).astype(jnp.bfloat16)
-    flipped = lax.dot_general(
-        pieces, reverse, (((2,), (1,)), ((), ())), preferred_element_type=jnp.float32
-    ).astype(jnp.bfloat16)
-    flipped = jnp.transpose(flipped, (0, 2, 1))
-    front = (lag_blocks - ahead) * windows
-    back = inner + lag_blocks * windows - front - depth
-    flipped = jnp.pad(flipped, ((0, 0), (0, 0), (front, back)))
-    receivers = jnp.concatenate(
-        [
-            flipped[:, :, (lag_blocks - k) * windows : (lag_blocks - k) * windows + inner]
-            for k in range(lag_blocks + 1)
-        ],
-        axis=1,
-    )
-    return correlate(picked, receivers, order, factor)
+    return correlate(pieces, local_channel.astype(jnp.int32), order, windows, factor)
 
 
 def solution(mesh):

time: 73.3 us -> 59.9 us (0.82)
  between operations: 7.69 us -> 0.03 us
  local copies, waits for them, and re-layouts: 4.82 us -> 1.44 us
  other arithmetic: 3.88 us -> 2.42 us
    convert_element_type x1, other arithmetic: 1.72 us -> 0.18 us  [whiten(): return (strain * lax.rsqrt(mean_square + 1e-06)).astype(jnp.bfloat16)]
    unnamed x5, local copies, waits for them, and re-layouts: 2.23 us -> 1.29 us
where the time goes in v3:
time: 59.9 us; the launch traced here: 59.3 us
  Pallas kernels  55.4 us (92%)
  other arithmetic  2.42 us (4%)
  local copies, waits for them, and re-layouts  1.44 us (2%)
    pallas_call x1, Pallas kernels, correlate(): pl.pallas_call(functools.partial(kernel, (chan_size, win_size, lag_blocks...  55.4 us
    reduce_sum x1, other arithmetic, whiten(): mean_square = jnp.mean(strain * strain, axis=-1, keepdims=True)  1.91 us
    unnamed x5, local copies, waits for them, and re-layouts  1.29 us

profile of v3, /device:TPU:0, one launch (start us, length us, event | category | flops | bytes accessed | tf_op | source)
XLA Modules:
  0.0 59.3 jit_solution(11600624327462642029)
XLA Ops:
  0.0 0.0 copy-start
  0.0 1.9 %multiply_reduce_fusion = f32[8,8]{1,0:T(8,128)S(1)} fusion(f32[8,8,7500]{2,1,0:T(8,128)} %param.2), kind=kLoop, calls=%fused_computation.1 | loop fusion | flops 959936 | bytes 1920256 | tf_op jit(solution)/shard_map/reduce_sum | solution.py:16
  1.9 0.2 copy-done
  2.1 0.0 copy-start.1
  2.1 0.2 multiply_convert_fusion
  2.3 0.1 pad_bitcast_fusion.pieces_ref
  2.4 0.4 copy-done.1
  2.8 0.1 reshape.91
  2.9 0.2 convert_reduce_fusion
  3.1 0.1 select_reduce_fusion.local_ref
  3.2 55.4 %shard_map.28 = f32[8,8,513]{2,1,0:T(8,128)S(1)} custom-call(bf16[8,480,128]{2,1,0:T(8,128)(2,1)S(1)} %pad_bitcast_fusion.pieces_ref, s32[4]{0:T(128)S(1)} %select_reduce_fusion.local_ref, s32[32]{0:T(128)S(1)} %multiply_add_fusion.order_ref), custom_call_target="tpu_custom_call" | custom-call | tf_op jit(solution)/shard_map/pallas_call | solution.py:179
  58.6 0.7 %copy.4 = f32[8,8,513]{2,1,0:T(8,128)} copy(f32[8,8,513]{2,1,0:T(8,128)S(1)} %shard_map.28) | data formatting | bytes 262656
  (4 shorter events, 0.0 us)
Async XLA Ops:
  0.0 2.1 %copy-start = (f32[8,8,7500]{2,1,0:T(8,128)S(1)}, f32[8,8,7500]{2,1,0:T(8,128)}, u32[]{:S(2)}) copy-start(f32[8,8,7500]{2,1,0:T(8,128)} %param.2) | copy-start | bytes 5760004
  2.1 0.7 %copy-start.1 = (s32[4,8]{1,0:T(4,128)S(1)}, s32[4,8]{1,0:T(4,128)}, u32[]{:S(2)}) copy-start(s32[4,8]{1,0:T(4,128)} %param.3) | copy-start | bytes 388

commit v4 on v3

--- a/solution.py
+++ b/solution.py
@@ -29,7 +29,7 @@
 
 
 def kernel(
-    sizes, factor, pieces_ref, local_ref, order_ref, out_ref,
+    sizes, streamed, factor, pieces_ref, local_ref, order_ref, out_ref,
     recv_ref, wide_ref, held_ref, probe_ref, partial_ref, send_ref, land_ref,
     send_sem, recv_sem, stack_send_sem, stack_recv_sem,
 ):
@@ -67,6 +67,17 @@
             send_sem=send_sem.at[way, step, item],
             recv_sem=recv_sem.at[way, step, item],
             device_id={"chan": targets[way]},
+            device_id_type=pl.DeviceIdType.MESH,
+        )
+
+    def stack_hop(dest, origin):
+        slot = lax.rem(dest - win + win_size, win_size) - 1
+        return pltpu.make_async_remote_copy(
+            src_ref=partial_ref.at[origin * per_shard + dest],
+            dst_ref=land_ref.at[slot, origin],
+            send_sem=stack_send_sem.at[dest, origin],
+            recv_sem=stack_recv_sem.at[slot, origin],
+            device_id={"win": jnp.int32(dest)},
             device_id_type=pl.DeviceIdType.MESH,
         )
 
@@ -91,6 +102,13 @@
                 totals.append(jnp.broadcast_to(last * factor, (1, BLOCK)))
                 place = origin * per_shard + way * count + item
                 partial_ref[place, channel : channel + 1, :] = jnp.concatenate(totals, axis=1)
+        if streamed:
+            for item in range(count):
+                dest = way * count + item
+
+                @pl.when(win != dest)
+                def _():
+                    stack_hop(dest, origin).start()
 
     for way in range(ways):
         for item in range(count):
@@ -135,6 +153,39 @@
                 hop(way, step, item).wait_send()
 
     per_win = out_ref.shape[0]
+    if streamed:
+        def arrived(index, carry):
+            for slot in range(win_size - 1):
+                peer = lax.rem(win + slot + 1, win_size)
+                pltpu.make_async_remote_copy(
+                    src_ref=partial_ref.at[index],
+                    dst_ref=land_ref.at[slot, index],
+                    send_sem=stack_send_sem.at[slot, index],
+                    recv_sem=stack_recv_sem.at[slot, index],
+                    device_id={"win": peer},
+                    device_id_type=pl.DeviceIdType.MESH,
+                ).wait_recv()
+            return carry
+
+        lax.fori_loop(0, chan_size, arrived, 0)
+        for item in range(per_win):
+            place = order_ref[win * per_win + item]
+            owner = lax.div(place, per_shard)
+            total = partial_ref[place]
+            for slot in range(win_size - 1):
+                total = total + land_ref[slot, owner]
+            out_ref[item] = total[:, : out_ref.shape[2]]
+
+        def sent(index, carry):
+            for dest in range(win_size):
+                @pl.when(win != dest)
+                def _():
+                    stack_hop(dest, index).wait_send()
+            return carry
+
+        lax.fori_loop(0, chan_size, sent, 0)
+        return
+
     for dest in range(win_size):
         for item in range(per_win):
             send_ref[dest, item] = partial_ref[order_ref[dest * per_win + item]]
@@ -162,7 +213,7 @@
         stack_copy(step).wait_send()
 
 
-def correlate(pieces, local_channel, order, windows, factor):
+def correlate(pieces, local_channel, order, windows, rounds, factor):
     channels, depth, _ = pieces.shape
     per_shard = local_channel.shape[0]
     total = order.shape[0]
@@ -174,10 +225,12 @@
     reach = -(-(inner + lag_blocks * windows) // BLOCK) * BLOCK
     lanes = (lag_blocks + 1) * BLOCK
     per_win = total // win_size
+    streamed = rounds == win_size and total // rounds == chan_size and per_shard == rounds
+    stack_copies = (win_size, chan_size) if streamed else (win_size - 1,)
     ways = 2 if per_shard % 2 == 0 else 1
     count = per_shard // ways
     return pl.pallas_call(
-        functools.partial(kernel, (chan_size, win_size, lag_blocks, windows, front), factor),
+        functools.partial(kernel, (chan_size, win_size, lag_blocks, windows, front), streamed, factor),
         out_shape=jax.ShapeDtypeStruct((per_win, channels, lag_count), jnp.float32),
         in_specs=[
             pl.BlockSpec(memory_space=pltpu.VMEM),
@@ -195,8 +248,8 @@
             pltpu.VMEM((win_size - 1, per_win, channels, lanes), jnp.float32),
             pltpu.SemaphoreType.DMA((ways, chan_size - 1, count)),
             pltpu.SemaphoreType.DMA((ways, chan_size - 1, count)),
-            pltpu.SemaphoreType.DMA((win_size - 1,)),
-            pltpu.SemaphoreType.DMA((win_size - 1,)),
+            pltpu.SemaphoreType.DMA(stack_copies),
+            pltpu.SemaphoreType.DMA(stack_copies),
         ],
         compiler_params=pltpu.CompilerParams(
             vmem_limit_bytes=48 * 1024 * 1024, collective_id=0, has_side_effects=True
@@ -231,7 +284,7 @@
     local_channel = jnp.sum(slot_pick * (flat_sources - me * channels)[None, :], axis=1)
     order = (owner * per_shard + rank).astype(jnp.int32)
 
-    return correlate(pieces, local_channel.astype(jnp.int32), order, windows, factor)
+    return correlate(pieces, local_channel.astype(jnp.int32), order, windows, rounds, factor)
 
 
 def solution(mesh):

time: 59.9 us -> 56.6 us (0.945)
  Pallas kernels: 55.4 us -> 52.6 us
    pallas_call x1, Pallas kernels: 55.4 us -> 52.6 us  [correlate(): pl.pallas_call(functools.partial(kernel, (chan_size, win_size, lag_blocks...]
where the time goes in v4:
time: 56.6 us; the launch traced here: 56.5 us
  Pallas kernels  52.6 us (93%)
  other arithmetic  2.42 us (4%)
  local copies, waits for them, and re-layouts  1.44 us (3%)
    pallas_call x1, Pallas kernels, correlate(): pl.pallas_call(functools.partial(kernel, (chan_size, win_size, lag_blocks...  52.6 us
    reduce_sum x1, other arithmetic, whiten(): mean_square = jnp.mean(strain * strain, axis=-1, keepdims=True)  1.91 us
    unnamed x5, local copies, waits for them, and re-layouts  1.29 us

profile of v4, /device:TPU:0, one launch (start us, length us, event | category | flops | bytes accessed | tf_op | source)
XLA Modules:
  0.0 56.5 jit_solution(14197029668077782779)
XLA Ops:
  0.0 0.0 copy-start
  0.0 1.9 %multiply_reduce_fusion = f32[8,8]{1,0:T(8,128)S(1)} fusion(f32[8,8,7500]{2,1,0:T(8,128)} %param.2), kind=kLoop, calls=%fused_computation.1 | loop fusion | flops 959936 | bytes 1920256 | tf_op jit(solution)/shard_map/reduce_sum | solution.py:16
  1.9 0.2 copy-done
  2.1 0.0 copy-start.1
  2.1 0.2 multiply_convert_fusion
  2.3 0.1 pad_bitcast_fusion.pieces_ref
  2.4 0.4 copy-done.1
  2.8 0.1 reshape.91
  2.9 0.2 convert_reduce_fusion
  3.1 0.1 select_reduce_fusion.local_ref
  3.2 52.6 %shard_map.28 = f32[8,8,513]{2,1,0:T(8,128)S(1)} custom-call(bf16[8,480,128]{2,1,0:T(8,128)(2,1)S(1)} %pad_bitcast_fusion.pieces_ref, s32[4]{0:T(128)S(1)} %select_reduce_fusion.local_ref, s32[32]{0:T(128)S(1)} %multiply_add_fusion.order_ref), custom_call_target="tpu_custom_call" | custom-call | tf_op jit(solution)/shard_map/pallas_call | solution.py:232
  55.8 0.7 %copy.4 = f32[8,8,513]{2,1,0:T(8,128)} copy(f32[8,8,513]{2,1,0:T(8,128)S(1)} %shard_map.28) | data formatting | bytes 262656
  (4 shorter events, 0.0 us)
Async XLA Ops:
  0.0 2.1 %copy-start = (f32[8,8,7500]{2,1,0:T(8,128)S(1)}, f32[8,8,7500]{2,1,0:T(8,128)}, u32[]{:S(2)}) copy-start(f32[8,8,7500]{2,1,0:T(8,128)} %param.2) | copy-start | bytes 5760004
  2.1 0.7 %copy-start.1 = (s32[4,8]{1,0:T(4,128)S(1)}, s32[4,8]{1,0:T(4,128)}, u32[]{:S(2)}) copy-start(s32[4,8]{1,0:T(4,128)} %param.3) | copy-start | bytes 388

commit v5 on v4

--- a/solution.py
+++ b/solution.py
@@ -30,7 +30,7 @@
 
 def kernel(
     sizes, streamed, factor, pieces_ref, local_ref, order_ref, out_ref,
-    recv_ref, wide_ref, held_ref, probe_ref, partial_ref, send_ref, land_ref,
+    recv_ref, wide_ref, held_ref, own_ref, probe_ref, partial_ref, send_ref, land_ref,
     send_sem, recv_sem, stack_send_sem, stack_recv_sem,
 ):
     chan_size, win_size, lag_blocks, windows, front = sizes
@@ -52,6 +52,7 @@
     for way in range(ways):
         for item in range(count):
             held_ref[way, 0, item] = pieces_ref[local_ref[way * count + item]]
+    own_ref[...] = jnp.zeros_like(own_ref)
     probe_ref[...] = jnp.zeros_like(probe_ref)
     pl.semaphore_wait(barrier, len(targets) + win_size - 1)
 
@@ -81,34 +82,40 @@
             device_id_type=pl.DeviceIdType.MESH,
         )
 
-    def work(way, step):
-        origin = here - step if way == 0 else here + step
-        origin = ring_index(lax.rem(origin + chan_size, chan_size), chan_size)
-        for item in range(count):
-            probe_ref[way, :depth, item * BLOCK : (item + 1) * BLOCK] = held_ref[way, step, item]
-        for channel in range(channels):
-            products = jnp.dot(recv_ref[channel], probe_ref[way], preferred_element_type=jnp.float32)
-            for item in range(count):
-                columns = products[:, item * BLOCK : (item + 1) * BLOCK]
-                parts = [columns[k * BLOCK : (k + 1) * BLOCK] for k in range(lag_blocks + 1)]
-                totals = []
-                for k in range(lag_blocks):
-                    mixed = jnp.where(later, parts[k], parts[k + 1])
-                    sheared = pltpu.roll(mixed, 0, 1, stride=1, stride_axis=0)
-                    total = jnp.sum(sheared, axis=0, keepdims=True)
-                    totals.append(pltpu.roll(total, 1, 1) * factor)
-                last = jnp.where(diagonal, parts[lag_blocks], 0.0)
-                last = jnp.sum(jnp.sum(last, axis=0, keepdims=True), axis=1, keepdims=True)
-                totals.append(jnp.broadcast_to(last * factor, (1, BLOCK)))
-                place = origin * per_shard + way * count + item
-                partial_ref[place, channel : channel + 1, :] = jnp.concatenate(totals, axis=1)
-        if streamed:
-            for item in range(count):
-                dest = way * count + item
-
-                @pl.when(win != dest)
-                def _():
-                    stack_hop(dest, origin).start()
+    def origin_of(way, step):
+        position = here - step if way == 0 else here + step
+        return ring_index(lax.rem(position + chan_size, chan_size), chan_size)
+
+    def load(probe, item, step):
+        for way in range(ways):
+            probe[item, :depth, way * BLOCK : (way + 1) * BLOCK] = held_ref[way, step, item]
+
+    def work(probe, item, step, channel):
+        products = jnp.dot(recv_ref[channel], probe[item], preferred_element_type=jnp.float32)
+        for way in range(ways):
+            columns = products[:, way * BLOCK : (way + 1) * BLOCK]
+            parts = [columns[k * BLOCK : (k + 1) * BLOCK] for k in range(lag_blocks + 1)]
+            totals = []
+            for k in range(lag_blocks):
+                mixed = jnp.where(later, parts[k], parts[k + 1])
+                sheared = pltpu.roll(mixed, 0, 1, stride=1, stride_axis=0)
+                total = jnp.sum(sheared, axis=0, keepdims=True)
+                totals.append(pltpu.roll(total, 1, 1) * factor)
+            last = jnp.where(diagonal, parts[lag_blocks], 0.0)
+            last = jnp.sum(jnp.sum(last, axis=0, keepdims=True), axis=1, keepdims=True)
+            totals.append(jnp.broadcast_to(last * factor, (1, BLOCK)))
+            place = origin_of(way, step) * per_shard + way * count + item
+            partial_ref[place, pl.ds(channel, 1), :] = jnp.concatenate(totals, axis=1)
+
+    def send_stacks(item, step):
+        if not streamed:
+            return
+        for way in range(ways):
+            dest = way * count + item
+
+            @pl.when(win != dest)
+            def _():
+                stack_hop(dest, origin_of(way, step)).start()
 
     for way in range(ways):
         for item in range(count):
@@ -128,25 +135,32 @@
             moved = pltpu.roll(flipped, reach - shift, 1) if shift else flipped
             recv_ref[channel, k * BLOCK : (k + 1) * BLOCK, :] = moved[:, :inner].astype(jnp.bfloat16)
 
-    slots = max(ways, count)
+    spread = chan_size - 1 if chan_size - 1 <= channels else 0
+    for item in range(count):
+        load(own_ref, item, 0)
+        for channel in range(channels - spread):
+            work(own_ref, item, 0, channel)
 
     def body(step, carry):
-        for slot in range(slots):
-            if slot < count:
-                for way in range(ways):
-                    hop(way, step - 1, slot).wait_recv()
-
-                    @pl.when(step < chan_size - 1)
-                    def _():
-                        hop(way, step, slot).start()
-
-            if slot < ways:
-                work(slot, step - 1)
+        for item in range(count):
+            for way in range(ways):
+                hop(way, step - 1, item).wait_recv()
+
+                @pl.when(step < chan_size - 1)
+                def _():
+                    hop(way, step, item).start()
+
+            load(probe_ref, item, step)
+            if spread:
+                work(own_ref, item, 0, channels - spread + step - 1)
+            for channel in range(channels):
+                work(probe_ref, item, step, channel)
+            send_stacks(item, step)
         return carry
 
     lax.fori_loop(1, chan_size, body, 0)
-    for way in range(ways):
-        work(way, chan_size - 1)
+    for item in range(count):
+        send_stacks(item, 0)
     for step in range(chan_size - 1):
         for way in range(ways):
             for item in range(count):
@@ -242,7 +256,8 @@
             pltpu.VMEM((channels, (lag_blocks + 1) * BLOCK, inner), jnp.bfloat16),
             pltpu.VMEM((2, reach, BLOCK), jnp.bfloat16),
             pltpu.VMEM((ways, chan_size, count, depth, BLOCK), jnp.bfloat16),
-            pltpu.VMEM((ways, inner, count * BLOCK), jnp.bfloat16),
+            pltpu.VMEM((count, inner, ways * BLOCK), jnp.bfloat16),
+            pltpu.VMEM((count, inner, ways * BLOCK), jnp.bfloat16),
             pltpu.VMEM((total, channels, lanes), jnp.float32),
             pltpu.VMEM((win_size, per_win, channels, lanes), jnp.float32),
             pltpu.VMEM((win_size - 1, per_win, channels, lanes), jnp.float32),

time: 56.6 us -> 54.3 us (0.959)
  Pallas kernels: 52.6 us -> 50.2 us
    pallas_call x1, Pallas kernels: 52.6 us -> 50.2 us  [correlate(): pl.pallas_call(functools.partial(kernel, (chan_size, win_size, lag_blocks...]
where the time goes in v5:
time: 54.3 us; the launch traced here: 54.1 us
  Pallas kernels  50.2 us (92%)
  other arithmetic  2.42 us (4%)
  local copies, waits for them, and re-layouts  1.44 us (3%)
    pallas_call x1, Pallas kernels, correlate(): pl.pallas_call(functools.partial(kernel, (chan_size, win_size, lag_blocks...  50.2 us
    reduce_sum x1, other arithmetic, whiten(): mean_square = jnp.mean(strain * strain, axis=-1, keepdims=True)  1.91 us
    unnamed x5, local copies, waits for them, and re-layouts  1.29 us

profile of v5, /device:TPU:0, one launch (start us, length us, event | category | flops | bytes accessed | tf_op | source)
XLA Modules:
  0.0 54.1 jit_solution(4679575577701453426)
XLA Ops:
  0.0 0.0 copy-start
  0.0 1.9 %multiply_reduce_fusion = f32[8,8]{1,0:T(8,128)S(1)} fusion(f32[8,8,7500]{2,1,0:T(8,128)} %param.2), kind=kLoop, calls=%fused_computation.1 | loop fusion | flops 959936 | bytes 1920256 | tf_op jit(solution)/shard_map/reduce_sum | solution.py:16
  1.9 0.2 copy-done
  2.1 0.0 copy-start.1
  2.1 0.2 multiply_convert_fusion
  2.3 0.1 pad_bitcast_fusion.pieces_ref
  2.4 0.4 copy-done.1
  2.8 0.1 reshape.91
  2.9 0.2 convert_reduce_fusion
  3.1 0.1 select_reduce_fusion.local_ref
  3.2 50.2 %shard_map.28 = f32[8,8,513]{2,1,0:T(8,128)S(1)} custom-call(bf16[8,480,128]{2,1,0:T(8,128)(2,1)S(1)} %pad_bitcast_fusion.pieces_ref, s32[4]{0:T(128)S(1)} %select_reduce_fusion.local_ref, s32[32]{0:T(128)S(1)} %multiply_add_fusion.order_ref), custom_call_target="tpu_custom_call" | custom-call | tf_op jit(solution)/shard_map/pallas_call | solution.py:246
  53.4 0.7 %copy.4 = f32[8,8,513]{2,1,0:T(8,128)} copy(f32[8,8,513]{2,1,0:T(8,128)S(1)} %shard_map.28) | data formatting | bytes 262656
  (4 shorter events, 0.0 us)
Async XLA Ops:
  0.0 2.1 %copy-start = (f32[8,8,7500]{2,1,0:T(8,128)S(1)}, f32[8,8,7500]{2,1,0:T(8,128)}, u32[]{:S(2)}) copy-start(f32[8,8,7500]{2,1,0:T(8,128)} %param.2) | copy-start | bytes 5760004
  2.1 0.7 %copy-start.1 = (s32[4,8]{1,0:T(4,128)S(1)}, s32[4,8]{1,0:T(4,128)}, u32[]{:S(2)}) copy-start(s32[4,8]{1,0:T(4,128)} %param.3) | copy-start | bytes 388

commit v6 on v5

--- a/solution.py
+++ b/solution.py
@@ -52,8 +52,6 @@
     for way in range(ways):
         for item in range(count):
             held_ref[way, 0, item] = pieces_ref[local_ref[way * count + item]]
-    own_ref[...] = jnp.zeros_like(own_ref)
-    probe_ref[...] = jnp.zeros_like(probe_ref)
     pl.semaphore_wait(barrier, len(targets) + win_size - 1)
 
     row = lax.broadcasted_iota(jnp.int32, (BLOCK, BLOCK), 0)
@@ -124,6 +122,8 @@
     reverse = jnp.where(diagonal, 1.0, 0.0).astype(jnp.bfloat16)
     inner = recv_ref.shape[2]
     reach = wide_ref.shape[1]
+    for scratch in (own_ref, probe_ref):
+        scratch[:, depth:, :] = jnp.zeros((count, inner - depth, ways * BLOCK), jnp.bfloat16)
     wide_ref[...] = jnp.zeros_like(wide_ref)
     for channel in range(channels):
         wide_ref[channel % 2, front : front + depth, :] = pieces_ref[channel]
@@ -143,6 +143,8 @@
 
     def body(step, carry):
         for item in range(count):
+            if spread:
+                work(own_ref, item, 0, channels - spread + step - 1)
             for way in range(ways):
                 hop(way, step - 1, item).wait_recv()
 
@@ -151,8 +153,6 @@
                     hop(way, step, item).start()
 
             load(probe_ref, item, step)
-            if spread:
-                work(own_ref, item, 0, channels - spread + step - 1)
             for channel in range(channels):
                 work(probe_ref, item, step, channel)
             send_stacks(item, step)

time: 54.3 us -> 54.6 us (level)
  no operation moved by 1% of the time
where the time goes in v6:
time: 54.6 us; the launch traced here: 54.4 us
  Pallas kernels  50.5 us (92%)
  other arithmetic  2.42 us (4%)
  local copies, waits for them, and re-layouts  1.44 us (3%)
    pallas_call x1, Pallas kernels, correlate(): pl.pallas_call(functools.partial(kernel, (chan_size, win_size, lag_blocks...  50.5 us
    reduce_sum x1, other arithmetic, whiten(): mean_square = jnp.mean(strain * strain, axis=-1, keepdims=True)  1.91 us
    unnamed x5, local copies, waits for them, and re-layouts  1.29 us

profile of v6, /device:TPU:0, one launch (start us, length us, event | category | flops | bytes accessed | tf_op | source)
XLA Modules:
  0.0 54.4 jit_solution(13032976262067796339)
XLA Ops:
  0.0 0.0 copy-start
  0.0 1.9 %multiply_reduce_fusion = f32[8,8]{1,0:T(8,128)S(1)} fusion(f32[8,8,7500]{2,1,0:T(8,128)} %param.2), kind=kLoop, calls=%fused_computation.1 | loop fusion | flops 959936 | bytes 1920256 | tf_op jit(solution)/shard_map/reduce_sum | solution.py:16
  1.9 0.2 copy-done
  2.1 0.0 copy-start.1
  2.1 0.2 multiply_convert_fusion
  2.3 0.1 pad_bitcast_fusion.pieces_ref
  2.4 0.4 copy-done.1
  2.8 0.1 reshape.91
  2.9 0.2 convert_reduce_fusion
  3.1 0.1 select_reduce_fusion.local_ref
  3.2 50.5 %shard_map.28 = f32[8,8,513]{2,1,0:T(8,128)S(1)} custom-call(bf16[8,480,128]{2,1,0:T(8,128)(2,1)S(1)} %pad_bitcast_fusion.pieces_ref, s32[4]{0:T(128)S(1)} %select_reduce_fusion.local_ref, s32[32]{0:T(128)S(1)} %multiply_add_fusion.order_ref), custom_call_target="tpu_custom_call" | custom-call | tf_op jit(solution)/shard_map/pallas_call | solution.py:246
  53.7 0.7 %copy.4 = f32[8,8,513]{2,1,0:T(8,128)} copy(f32[8,8,513]{2,1,0:T(8,128)S(1)} %shard_map.28) | data formatting | bytes 262656
  (4 shorter events, 0.0 us)
Async XLA Ops:
  0.0 2.1 %copy-start = (f32[8,8,7500]{2,1,0:T(8,128)S(1)}, f32[8,8,7500]{2,1,0:T(8,128)}, u32[]{:S(2)}) copy-start(f32[8,8,7500]{2,1,0:T(8,128)} %param.2) | copy-start | bytes 5760004
  2.1 0.7 %copy-start.1 = (s32[4,8]{1,0:T(4,128)S(1)}, s32[4,8]{1,0:T(4,128)}, u32[]{:S(2)}) copy-start(s32[4,8]{1,0:T(4,128)} %param.3) | copy-start | bytes 388
